TPU v7x, 256 devices: a whole 4x4x8 slice. The times are simulated.
256 devices in a mesh: grp: 4 (over x_lo, core), blk: 64 (over z, y, x_hi).
Axes of the slice: x: 4 (x_hi: 2, x_lo: 2; x = x_hi * 2 + x_lo), y: 4, z: 8, core: 2. Of those that a mesh axis runs over, the one named last changes fastest.
Arguments:
- mem_keys: bfloat16 [1048576, 128], P(('grp', 'blk'))
- mem_values: bfloat16 [1048576, 512], P(('grp', 'blk'))
- offsets: int32 [4, 64], P('grp', 'blk'), may hold values from 0 to 2048, as said below
- block_skip: int32 [4, 64], P('grp', 'blk'), may hold values from 0 to 63, as said below
- queries: bfloat16 [65536, 128], P('blk')
Outputs:
- retrieved: bfloat16 [65536, 512], P('blk', 'grp')
Inputs may be any that keep to these rules, and one draw needn't show every extreme that they name: `offsets`: each window lies inside its device's resident rows. block_skip[g, j] names one of the blocks that attend to slab (g, j), and every query block is named by fewer than all of the slabs it attends to.
All inputs are finite; a program needn't handle non-finite values.
Results may differ from a plain program's by a relative error of at most 0.0048.
Values may be sent and summed in bfloat16 or wider, within the bound.
A program may use at most 192 MiB of HBM per device.

v0:
```python
import jax
import jax.numpy as jnp
from jax import lax
from jax.sharding import PartitionSpec as P

STEPS = 4


lowest = -1e30


def combined_all(value, axis, join):
    pieces = jax.tree.map(lambda part: lax.all_gather(part, axis), value)
    head = jax.tree.map(lambda part: part[0], pieces)
    tail = jax.tree.map(lambda part: part[1:], pieces)
    running, _ = lax.scan(lambda running, piece: (join(running, piece), None), head, tail)
    return running


def shifted(block, axis, distance):
    devices = range(lax.axis_size(axis))
    route = [((i - distance) % len(devices), i) for i in devices]
    return lax.ppermute(block, axis, route)


def slab_partial(block, keys_w, vals_w, scale):
    scores = (
        lax.dot_general(block, keys_w, (((1,), (1,)), ((), ())), preferred_element_type=jnp.float32)
        * scale
    )
    top = jnp.max(scores, axis=1)
    prob = jnp.exp(scores - top[:, None])
    total = jnp.sum(prob, axis=1)
    acc = jnp.dot(prob.astype(jnp.bfloat16), vals_w, preferred_element_type=jnp.float32)
    return (top, total, acc)


def join(first, second):
    top = jnp.maximum(first[0], second[0])
    fa = jnp.exp(first[0] - top)
    fb = jnp.exp(second[0] - top)
    return (
        top,
        first[1] * fa + second[1] * fb,
        first[2] * fa[..., None] + second[2] * fb[..., None],
    )


def group_combine(state):
    groups = lax.axis_size("grp")
    width = state[2].shape[2]
    share = width // groups
    top, total, acc = combined_all(state, "grp", join)
    part_acc = lax.dynamic_slice_in_dim(acc, lax.axis_index("grp") * share, share, 2)
    return (top, total, part_acc)


def body(mem_keys, mem_values, offsets, block_skip, queries):
    cycle = lax.axis_size("blk")
    here = lax.axis_index("blk")
    window = mem_keys.shape[0] // 2
    start = offsets[0, 0]
    keys_w = lax.dynamic_slice_in_dim(mem_keys, start, window, 0)
    vals_w = lax.dynamic_slice_in_dim(mem_values, start, window, 0)
    skipped = block_skip[0, 0]
    rows = queries.shape[0]
    width = mem_values.shape[1]
    scale = queries.shape[1] ** (-0.5)
    moving = queries.astype(jnp.float32)
    state = (
        jnp.full((rows,), lowest, jnp.float32),
        jnp.zeros((rows,), jnp.float32),
        jnp.zeros((rows, width), jnp.float32),
    )
    for step in range(STEPS):
        visit_top, visit_total, visit_acc = slab_partial(
            moving.astype(jnp.bfloat16), keys_w, vals_w, scale
        )
        keep = skipped != (here - step) % cycle
        state = join(
            state,
            (
                jnp.where(keep, visit_top, lowest),
                jnp.where(keep, visit_total, 0.0),
                jnp.where(keep, visit_acc, 0.0),
            ),
        )
        if step + 1 < STEPS:
            moving, top, total, acc = shifted((moving, state[0], state[1], state[2]), "blk", 1)
            state = (top, total, acc)
    state = shifted((state[0], state[1], state[2]), "blk", 1 - STEPS)
    top, total, acc = group_combine((state[0][None], state[1][None], state[2][None]))
    final = (top[0], total[0], acc[0])
    ratio = final[2] / final[1][:, None]
    squares = lax.psum(jnp.sum(ratio * ratio, axis=1), "grp")
    return (ratio * lax.rsqrt(squares / width + 1e-06)[:, None]).astype(jnp.bfloat16)


def solution(mesh):
    placed = (
        P(("grp", "blk"), None),
        P(("grp", "blk"), None),
        P("grp", "blk"),
        P("grp", "blk"),
        P("blk", None),
    )
    return jax.shard_map(
        body, mesh=mesh, in_specs=placed, out_specs=P("blk", "grp"), check_vma=False
    )
```

profile of v0, /device:TPU:1, one launch (start us, length us, event | category | flops | bytes accessed | tf_op | source)
XLA Modules:
  0.0 358.5 jit_solution(8600184545669260732)
XLA Ops:
  7.9 2.2 multiply_reduce_fusion.3
  10.2 1.4 fusion.4
  11.6 0.7 copy-done.5
  12.4 3.8 %multiply_add_fusion.3 = f32[1024,512]{1,0:T(8,128)} fusion(f32[2048,1024]{1,0:T(8,128)S(1)} %get-tuple-element.100, f32[1024]{0:T(1024)S(1)} %get-tuple-element.99, bf16[4096,512]{1,0:T(8,128)(2,1)S(1)} %copy-done.5, s32[]{:T(128)S(6)} %select_n.103, f32[1024]{0:T(1024)S(1)} %get-tuple-element.91, f32[1024]{0:T(1024)S(1)} %get-tuple-element.89, pred[]{:T(512)S(6)} %ne.31), kind=kOutput, calls=%fused_computation.40 | convolution fusion | flops 2155347968 | bytes 12595205 | tf_op jit(solution)/shard_map/dot_general | solution.py:34
  16.2 3.5 collective-permute-start.11
  19.7 1.3 collective-permute-start.1
  21.0 2.7 collective-permute-start
  23.7 1.2 collective-permute-start.7
  24.9 53.8 %collective-permute-done.1 = bf16[1024,128]{1,0:T(8,128)(2,1)} collective-permute-done((bf16[1024,128]{1,0:T(8,128)(2,1)S(1)}, bf16[1024,128]{1,0:T(8,128)(2,1)}, u32[]{:S(2)}, u32[]{:S(2)}) %collective-permute-start.1) | collective-permute-done | bytes 262176 | tf_op jit(solution)/shard_map/ppermute | solution.py:23
  78.8 2.2 multiply_reduce_fusion.2
  81.0 1.4 fusion.6
  82.4 0.3 collective-permute-start.3
  82.7 0.4 copy-done.6
  83.2 5.2 %multiply_add_fusion.2 = f32[1024,512]{1,0:T(8,128)} fusion(f32[1024,512]{1,0:T(8,128)} %collective-permute-done.11, f32[1024]{0:T(1024)S(1)} %get-tuple-element.87, f32[1024]{0:T(1024)S(1)} %get-tuple-element.86, pred[]{:T(512)S(6)} %ne.33, bf16[4096,512]{1,0:T(8,128)(2,1)S(1)} %copy-done.6, s32[]{:T(128)S(6)} %select_n.103, ...), kind=kOutput, calls=%fused_computation.39 | convolution fusion | flops 2155872256 | bytes 14692357 | tf_op jit(solution)/shard_map/dot_general | solution.py:34
  88.4 0.6 collective-permute-start.8
  89.0 6.1 %collective-permute-done.3 = bf16[1024,128]{1,0:T(8,128)(2,1)S(1)} collective-permute-done((bf16[1024,128]{1,0:T(8,128)(2,1)}, bf16[1024,128]{1,0:T(8,128)(2,1)S(1)}, u32[]{:S(2)}, u32[]{:S(2)}) %collective-permute-start.3) | collective-permute-done | bytes 262176 | tf_op jit(solution)/shard_map/ppermute | solution.py:23
  95.1 1.3 multiply_reduce_fusion.1
  96.4 1.4 fusion.8
  97.9 42.3 %collective-permute-done.2 = f32[1024]{0:T(1024)S(1)} collective-permute-done((f32[1024]{0:T(1024)S(1)}, f32[1024]{0:T(1024)S(1)}, u32[]{:S(2)}, u32[]{:S(2)}) %collective-permute-start.2) | collective-permute-done | bytes 4128 | tf_op jit(solution)/shard_map/ppermute | solution.py:23
  140.2 0.1 collective-permute-done.8
  140.3 2.4 fusion.13
  142.8 1.3 copy-done.2
  144.1 1.9 multiply_add_fusion.1
  146.1 0.1 collective-permute-start.13
  146.3 0.3 collective-permute-start.9
  146.6 2.2 multiply_reduce_fusion
  148.8 1.4 fusion.10
  150.3 44.9 %collective-permute-done.4 = f32[1024]{0:T(1024)S(1)} collective-permute-done((f32[1024]{0:T(1024)S(1)}, f32[1024]{0:T(1024)S(1)}, u32[]{:S(2)}, u32[]{:S(2)}) %collective-permute-start.4) | collective-permute-done | bytes 4128 | tf_op jit(solution)/shard_map/ppermute | solution.py:23
  195.2 0.1 collective-permute-done.9
  195.3 2.5 fusion.11
  197.8 1.9 multiply_add_fusion
  199.8 44.6 %collective-permute-done.14 = f32[1024,512]{1,0:T(8,128)S(1)} collective-permute-done((f32[1024,512]{1,0:T(8,128)S(1)}, f32[1024,512]{1,0:T(8,128)S(1)}, u32[]{:S(2)}, u32[]{:S(2)}) %collective-permute-start.14) | collective-permute-done | bytes 2097184 | tf_op jit(solution)/shard_map/ppermute | solution.py:23
  244.4 1.4 copy-done.3
  245.8 4.0 %collective-permute-start.6 = (f32[1024]{0:T(1024)S(1)}, f32[1024]{0:T(1024)S(1)}, u32[]{:S(2)}, u32[]{:S(2)}) collective-permute-start(f32[1024]{0:T(1024)S(1)} %get-tuple-element.80), channel_id=1, source_target_pairs={{3,0},{4,1},{5,2},{6,3},{7,4},{8,5},{9,6},{10,7},{11,8},{12,9},{13... | collective-permute-start | bytes 12296 | tf_op jit(solution)/shard_map/ppermute | solution.py:23
  249.7 0.1 collective-permute-start.10
  249.8 0.9 collective-permute-done.6
  250.7 12.0 %all-gather = f32[4096]{0:T(1024)S(1)} all-gather(f32[1024]{0:T(1024)S(1)} %collective-permute-done.6), channel_id=2, replica_groups=mesh['grp'=4,'blk'=64] {'grp'}, dimensions={0}, use_global_device_ids=true | all-gather | bytes 20480 | tf_op jit(solution)/shard_map/all_gather | solution.py:13
  262.7 5.2 %all-gather.1 = f32[4096]{0:T(1024)S(1)} all-gather(f32[1024]{0:T(1024)S(1)} %collective-permute-done.10), channel_id=3, replica_groups=mesh['grp'=4,'blk'=64] {'grp'}, dimensions={0}, use_global_device_ids=true | all-gather | bytes 20480 | tf_op jit(solution)/shard_map/all_gather | solution.py:13
  267.9 62.6 %all-gather.5.cloned.1.call-done = f32[4096,512]{1,0:T(8,128)} async-done(((f32[1024,512]{1,0:T(8,128)}), f32[4096,512]{1,0:T(8,128)}) %all-gather.5.cloned.1.call-update) | async-done | bytes 8388624 | tf_op jit(solution)/shard_map/all_gather | solution.py:13
  330.5 6.2 %slice.35 = f32[3072,512]{1,0:T(8,128)} slice(f32[4096,512]{1,0:T(8,128)} %all-gather.5.cloned.1.call-done), slice={[1024:4096], [0:512]} | slice | bytes 12582912 | tf_op jit(solution)/shard_map/slice | solution.py:15
  336.7 1.8 slice_bitcast_fusion
  338.5 6.6 %while.14 = (s32[]{:T(128)}, f32[1,1024]{1,0:T(1,128)S(1)}, f32[1,1024]{1,0:T(1,128)S(1)}, f32[1,1024,512]{2,1,0:T(8,128)S(1)}, f32[3,1,1024]{2,1,0:T(1,128)S(1)...) while((s32[]{:T(128)}, f32[1,1024]{1,0:T(1,128)S(1)}, f32[1,1024]{1,0:T(1,128)S(1)}, ...), condition=%wide.region_9.10_spmd, body=%wide.region_8.9_spmd.sunk | while | flops 1579010 | bytes 6332509 | solution.py:16
  338.5 2.1 fusion.68
  340.7 2.1 fusion.68
  342.9 2.1 fusion.68
  345.1 0.4 multiply_reduce_fusion.4
  345.4 5.1 %psum.7 = f32[1024]{0:T(1024)S(1)} all-reduce(f32[1024]{0:T(1024)S(1)} %multiply_reduce_fusion.4), channel_id=1, replica_groups=mesh['grp'=4,'blk'=64] {'grp'}, use_global_device_ids=true, to_apply=%region_11.12 | all-reduce | flops 1024 | bytes 8192 | tf_op jit(solution)/shard_map/psum | solution.py:95
  350.6 1.0 multiply_convert_fusion
  (40 shorter events, 0.5 us)
Async XLA Ops:
  6.5 1.4 copy-start
  6.5 324.0 %all-gather.5.cloned.1.call-start = ((), (), s32[]{:S(2)}) async-start(), calls=%async_computation | async-start | bytes 10485760 | tf_op jit(solution)/shard_map/all_gather | solution.py:13
  10.2 2.2 copy-start.5
  12.4 7.3 %copy-start.4 = (bf16[1024,128]{1,0:T(8,128)(2,1)S(1)}, bf16[1024,128]{1,0:T(8,128)(2,1)}, u32[]{:S(2)}) copy-start(bf16[1024,128]{1,0:T(8,128)(2,1)} %param.11) | copy-start | bytes 786436
  16.2 66.6 %collective-permute-start.11 = (f32[1024,512]{1,0:T(8,128)}, f32[1024,512]{1,0:T(8,128)}, u32[]{:S(2)}, u32[]{:S(2)}) collective-permute-start(f32[1024,512]{1,0:T(8,128)} %multiply_add_fusion.3), channel_id=1, source_target_pairs={{63,0},{0,1},{1,2},{2,3},{3,4},{4,5},{5,6},{6,7},{7,8},{8,9},{9,10... | collective-permute-start | bytes 6291464 | tf_op jit(solution)/shard_map/ppermute | solution.py:23
  19.7 59.1 %collective-permute-start.1 = (bf16[1024,128]{1,0:T(8,128)(2,1)S(1)}, bf16[1024,128]{1,0:T(8,128)(2,1)}, u32[]{:S(2)}, u32[]{:S(2)}) collective-permute-start(bf16[1024,128]{1,0:T(8,128)(2,1)S(1)} %copy-done.4), channel_id=1, source_target_pairs={{63,0},{0,1},{1,2},{2,3},{3,4},{4,5},{5,6},{6,7},{7,8},{8,9},{9,10... | collective-permute-start | bytes 786440 | tf_op jit(solution)/shard_map/ppermute | solution.py:23
  21.0 61.7 %collective-permute-start = (f32[1024]{0:T(1024)S(1)}, f32[1024]{0:T(1024)S(1)}, u32[]{:S(2)}, u32[]{:S(2)}) collective-permute-start(f32[1024]{0:T(1024)S(1)} %get-tuple-element.92), channel_id=1, source_target_pairs={{63,0},{0,1},{1,2},{2,3},{3,4},{4,5},{5,6},{6,7},{7,8},{8,9},{9,10... | collective-permute-start | bytes 12296 | tf_op jit(solution)/shard_map/ppermute | solution.py:23
  23.7 59.0 %collective-permute-start.7 = (f32[1024]{0:T(1024)S(1)}, f32[1024]{0:T(1024)S(1)}, u32[]{:S(2)}, u32[]{:S(2)}) collective-permute-start(f32[1024]{0:T(1024)S(1)} %get-tuple-element.90), channel_id=1, source_target_pairs={{63,0},{0,1},{1,2},{2,3},{3,4},{4,5},{5,6},{6,7},{7,8},{8,9},{9,10... | collective-permute-start | bytes 12296 | tf_op jit(solution)/shard_map/ppermute | solution.py:23
  81.0 2.2 copy-start.6
  82.4 12.7 %collective-permute-start.3 = (bf16[1024,128]{1,0:T(8,128)(2,1)}, bf16[1024,128]{1,0:T(8,128)(2,1)S(1)}, u32[]{:S(2)}, u32[]{:S(2)}) collective-permute-start(bf16[1024,128]{1,0:T(8,128)(2,1)} %collective-permute-done.1), channel_id=1, source_target_pairs={{63,0},{0,1},{1,2},{2,3},{3,4},{4,5},{5,6},{6,7},{7,8},{8,9},{9,10... | collective-permute-start | bytes 786440 | tf_op jit(solution)/shard_map/ppermute | solution.py:23
  88.4 54.4 %collective-permute-start.12 = (f32[1024,512]{1,0:T(8,128)}, f32[1024,512]{1,0:T(8,128)S(1)}, u32[]{:S(2)}, u32[]{:S(2)}) collective-permute-start(f32[1024,512]{1,0:T(8,128)} %multiply_add_fusion.2), channel_id=1, source_target_pairs={{63,0},{0,1},{1,2},{2,3},{3,4},{4,5},{5,6},{6,7},{7,8},{8,9},{9,10... | collective-permute-start | bytes 6291464 | tf_op jit(solution)/shard_map/ppermute | solution.py:23
  88.4 51.9 %collective-permute-start.2 = (f32[1024]{0:T(1024)S(1)}, f32[1024]{0:T(1024)S(1)}, u32[]{:S(2)}, u32[]{:S(2)}) collective-permute-start(f32[1024]{0:T(1024)S(1)} %get-tuple-element.88), channel_id=1, source_target_pairs={{63,0},{0,1},{1,2},{2,3},{3,4},{4,5},{5,6},{6,7},{7,8},{8,9},{9,10... | collective-permute-start | bytes 12296 | tf_op jit(solution)/shard_map/ppermute | solution.py:23
  88.4 51.9 %collective-permute-start.8 = (f32[1024]{0:T(1024)S(1)}, f32[1024]{0:T(1024)S(1)}, u32[]{:S(2)}, u32[]{:S(2)}) collective-permute-start(f32[1024]{0:T(1024)S(1)} %get-tuple-element.85), channel_id=1, source_target_pairs={{63,0},{0,1},{1,2},{2,3},{3,4},{4,5},{5,6},{6,7},{7,8},{8,9},{9,10... | collective-permute-start | bytes 12296 | tf_op jit(solution)/shard_map/ppermute | solution.py:23
  96.4 44.0 %copy-start.7 = (bf16[4096,512]{1,0:T(8,128)(2,1)S(1)}, bf16[4096,512]{1,0:T(8,128)(2,1)}, u32[]{:S(2)}) copy-start(bf16[4096,512]{1,0:T(8,128)(2,1)} %param.8) | copy-start | bytes 12582916
  97.8 48.8 %collective-permute-start.5 = (bf16[1024,128]{1,0:T(8,128)(2,1)S(1)}, bf16[1024,128]{1,0:T(8,128)(2,1)}, u32[]{:S(2)}, u32[]{:S(2)}) collective-permute-start(bf16[1024,128]{1,0:T(8,128)(2,1)S(1)} %collective-permute-done.3), channel_id=1, source_target_pairs={{63,0},{0,1},{1,2},{2,3},{3,4},{4,5},{5,6},{6,7},{7,8},{8,9},{9,10... | collective-permute-start | bytes 786440 | tf_op jit(solution)/shard_map/ppermute | solution.py:23
  142.8 1.3 copy-start.2
  146.1 51.7 %collective-permute-start.13 = (f32[1024,512]{1,0:T(8,128)S(1)}, f32[1024,512]{1,0:T(8,128)}, u32[]{:S(2)}, u32[]{:S(2)}) collective-permute-start(f32[1024,512]{1,0:T(8,128)S(1)} %multiply_add_fusion.1), channel_id=1, source_target_pairs={{63,0},{0,1},{1,2},{2,3},{3,4},{4,5},{5,6},{6,7},{7,8},{8,9},{9,10... | collective-permute-start | bytes 6291464 | tf_op jit(solution)/shard_map/ppermute | solution.py:23
  146.2 49.0 %collective-permute-start.4 = (f32[1024]{0:T(1024)S(1)}, f32[1024]{0:T(1024)S(1)}, u32[]{:S(2)}, u32[]{:S(2)}) collective-permute-start(f32[1024]{0:T(1024)S(1)} %get-tuple-element.84), channel_id=1, source_target_pairs={{63,0},{0,1},{1,2},{2,3},{3,4},{4,5},{5,6},{6,7},{7,8},{8,9},{9,10... | collective-permute-start | bytes 12296 | tf_op jit(solution)/shard_map/ppermute | solution.py:23
  146.3 49.0 %collective-permute-start.9 = (f32[1024]{0:T(1024)S(1)}, f32[1024]{0:T(1024)S(1)}, u32[]{:S(2)}, u32[]{:S(2)}) collective-permute-start(f32[1024]{0:T(1024)S(1)} %get-tuple-element.81), channel_id=1, source_target_pairs={{63,0},{0,1},{1,2},{2,3},{3,4},{4,5},{5,6},{6,7},{7,8},{8,9},{9,10... | collective-permute-start | bytes 12296 | tf_op jit(solution)/shard_map/ppermute | solution.py:23
  148.8 46.5 %copy-start.8 = (bf16[4096,512]{1,0:T(8,128)(2,1)S(1)}, bf16[4096,512]{1,0:T(8,128)(2,1)}, u32[]{:S(2)}) copy-start(bf16[4096,512]{1,0:T(8,128)(2,1)} %param.8) | copy-start | bytes 12582916
  199.7 44.7 %collective-permute-start.14 = (f32[1024,512]{1,0:T(8,128)S(1)}, f32[1024,512]{1,0:T(8,128)S(1)}, u32[]{:S(2)}, u32[]{:S(2)}) collective-permute-start(f32[1024,512]{1,0:T(8,128)S(1)} %multiply_add_fusion), channel_id=1, source_target_pairs={{3,0},{4,1},{5,2},{6,3},{7,4},{8,5},{9,6},{10,7},{11,8},{12,9},{13... | collective-permute-start | bytes 6291464 | tf_op jit(solution)/shard_map/ppermute | solution.py:23
  244.4 1.4 copy-start.3
  245.8 4.9 %collective-permute-start.6 = (f32[1024]{0:T(1024)S(1)}, f32[1024]{0:T(1024)S(1)}, u32[]{:S(2)}, u32[]{:S(2)}) collective-permute-start(f32[1024]{0:T(1024)S(1)} %get-tuple-element.80), channel_id=1, source_target_pairs={{3,0},{4,1},{5,2},{6,3},{7,4},{8,5},{9,6},{10,7},{11,8},{12,9},{13... | collective-permute-start | bytes 12296 | tf_op jit(solution)/shard_map/ppermute | solution.py:23
  249.7 12.9 %collective-permute-start.10 = (f32[1024]{0:T(1024)S(1)}, f32[1024]{0:T(1024)S(1)}, u32[]{:S(2)}, u32[]{:S(2)}) collective-permute-start(f32[1024]{0:T(1024)S(1)} %get-tuple-element.77), channel_id=1, source_target_pairs={{3,0},{4,1},{5,2},{6,3},{7,4},{8,5},{9,6},{10,7},{11,8},{12,9},{13... | collective-permute-start | bytes 12296 | tf_op jit(solution)/shard_map/ppermute | solution.py:23
  345.1 6.6 %copy-start.1 = (bf16[4096,128]{1,0:T(8,128)(2,1)S(1)}, bf16[4096,128]{1,0:T(8,128)(2,1)}, u32[]{:S(2)}) copy-start(bf16[4096,128]{1,0:T(8,128)(2,1)} %param.7) | copy-start | bytes 3145732
Sparse Core Ops, SparseCore 0:
  245.9 84.5 all-gather.4
where the time goes:
time: 359 us; the launch traced here: 358 us
  waiting for transfers between devices  255 us (71%)
  blocking collectives  22.3 us (6%)
  matrix products  21.8 us (6%)
  other arithmetic  17.6 us (5%)
  between operations  15.1 us (4%)
  starting transfers between devices  14.4 us (4%)
  local copies, waits for them, and re-layouts  11.8 us (3%)
    ppermute x15, waiting for transfers between devices, shifted(): return lax.ppermute(block, axis, route)  193 us
    all_gather x1, waiting for transfers between devices, combined_all(): pieces = jax.tree.map(lambda part: lax.all_gather(part, axis), value)  62.6 us
    all_gather x2, blocking collectives, combined_all(): pieces = jax.tree.map(lambda part: lax.all_gather(part, axis), value)  17.2 us
    ppermute x15, starting transfers between devices, shifted(): return lax.ppermute(block, axis, route)  14.4 us
    dot_general x4, matrix products, slab_partial(): jnp.dot(prob.astype(jnp.bfloat16), vals_w, preferred_element_type=jnp.flo...  13.9 us
    add x5, other arithmetic, join(): first[2] * fa[..., None] + second[2] * fb[..., None]  10.3 us
    dot_general x4, matrix products, slab_partial(): lax.dot_general(block, keys_w, (((1,), (1,)), ((), ())), preferred_elemen...  7.9 us
  transfers between devices with their start and end apart: 16, of which 9 were waited for; matrix products, arithmetic and copies ran while one was open for 6% of the time, Pallas kernels for 0%

commit v1 on v0

v1 whole, which is shorter than its diff:
```python
import functools

import jax
import jax.numpy as jnp
from jax import lax
from jax.experimental import pallas as pl
from jax.experimental.pallas import tpu as pltpu
from jax.sharding import PartitionSpec as P

MESH = pl.DeviceIdType.MESH
LOG2E = 1.4426950408889634
LOWEST = -1e30
HIGHEST = 3e38
TILES = 4
STEPS = 4
VISITS = TILES * STEPS
PAIR_LAG = 3
ITERS = 23


def joined(a, ms_a, b, ms_b):
    ma, la = ms_a[0:1, :], ms_a[1:2, :]
    mb, lb = ms_b[0:1, :], ms_b[1:2, :]
    top = jnp.maximum(ma, mb)
    fa = jnp.exp2(ma - top)
    fb = jnp.exp2(mb - top)
    total = la * fa + lb * fb
    return [x * fa + y.astype(jnp.float32) * fb for x, y in zip(a, b)], top, total


def kernel(
    skip_ref, k_ref, v_ref, q_ref, out_ref,
    vt, qs, own, own_ms, keep, keep_ms, hold, hold_ms, home, home_ms, ratio,
    cs, cs_ms, cr, cr_ms, ps, ps_ms, pr, pr_ms,
    xs, xs_ms, xr, xr_ms, ys, ys_ms, yr, yr_ms, ss, sr,
    q_send, q_recv, f_send, f_recv,
    send_sem, c_recv, p_recv, x_recv, y_recv, s_recv,
):
    g = lax.axis_index("grp")
    j = lax.axis_index("blk")
    nb = lax.axis_size("blk")
    core = lax.rem(g, 2)
    xl = lax.div(g, 2)
    xh = lax.rem(j, 2)
    g_core = g + 1 - 2 * core
    g_pair = lax.rem(g + 2, 4)
    g_both = g_core + 2 - 4 * xl

    def at(d):
        return lax.rem(j + nb + d, nb)

    cross = (g_pair, at(1 - 2 * xh))
    down = (g, at(-2))
    rows = q_ref.shape[0]
    tq = rows // TILES
    half = rows // 2
    width = v_ref.shape[1]
    scale = q_ref.shape[1] ** (-0.5) * LOG2E

    barrier = pltpu.get_barrier_semaphore()
    partners = [
        (g_core, j), (g_pair, j), (g_both, j), (g, at(2)), (g, at(-2)),
        (g_pair, at(1)), (g_pair, at(-1)), (g_pair, at(3)), (g_pair, at(-3)),
    ]
    for partner in partners:
        pl.semaphore_signal(barrier, inc=1, device_id=partner, device_id_type=MESH)
    pl.semaphore_wait(barrier, len(partners))

    def remote(src, dst, send, recv, device):
        return pltpu.make_async_remote_copy(
            src_ref=src, dst_ref=dst, send_sem=send, recv_sem=recv,
            device_id=device, device_id_type=MESH,
        )

    mine = pl.ds(core * half, half)
    theirs = pl.ds((1 - core) * half, half)

    def q_copy(step, device):
        return remote(
            q_ref.at[mine], qs.at[step, mine], q_send.at[step], q_recv.at[step], device
        )

    def q_forward(step):
        return remote(
            qs.at[step, mine], qs.at[step, mine], f_send.at[step], f_recv.at[step], (g_core, j)
        )

    q_out = [None, q_copy(1, (g, at(2))), q_copy(2, (g_pair, at(3))), q_copy(3, (g_pair, at(1)))]
    q_out[1].start()
    q_out[2].start()
    q_out[3].start()

    qs[0] = q_ref[...]
    for q in range(4):
        spot = 2 * lax.rem(core + q % 2, 2) + q // 2
        vt[spot] = v_ref[:, q * 128 : (q + 1) * 128].T

    def two(data_src, ms_src, data_dst, ms_dst, sem, recv, device):
        remote(data_src, data_dst, send_sem.at[2 * sem], recv.at[0], device).start()
        remote(ms_src, ms_dst, send_sem.at[2 * sem + 1], recv.at[1], device).start()

    def arrived(data, ms, recv):
        pltpu.make_async_copy(data, data, recv.at[0]).wait()
        pltpu.make_async_copy(ms, ms, recv.at[1]).wait()

    def send_cross(res, top, total, slot):
        xs[slot] = res.astype(jnp.bfloat16)
        xs_ms[slot, 0:1, :] = top
        xs_ms[slot, 1:2, :] = total
        two(xs.at[slot], xs_ms.at[slot], xr.at[slot], xr_ms.at[slot], 2, x_recv.at[slot], cross)

    def send_down(res, top, total, slot):
        ys[slot] = res.astype(jnp.bfloat16)
        ys_ms[slot, 0:1, :] = top
        ys_ms[slot, 1:2, :] = total
        two(ys.at[slot], ys_ms.at[slot], yr.at[slot], yr_ms.at[slot], 3, y_recv.at[slot], down)

    def compute(n):
        step = lax.div(n, TILES)
        tile = lax.rem(n, TILES)
        shift = jnp.where(step == 0, 0, jnp.where(step == 1, 2, jnp.where(step == 2, 3, 1)))
        block = lax.rem(j + nb - shift, nb)
        kept = skip_ref[0, 0] != block
        q = qs[step, pl.ds(pl.multiple_of(tile * tq, tq), tq), :]
        s = lax.dot_general(
            k_ref[...], q, (((1,), (1,)), ((), ())), preferred_element_type=jnp.float32
        )
        top = jnp.max(s, axis=0, keepdims=True)
        ref = jnp.where(kept, top, HIGHEST)
        p = jnp.exp2((s - ref) * scale)
        total = jnp.sum(p, axis=0, keepdims=True)
        acc = jnp.dot(
            vt[...].reshape(width, vt.shape[2]), p.astype(jnp.bfloat16),
            preferred_element_type=jnp.float32,
        )
        own[n, 0] = acc[0:128]
        own[n, 1] = acc[128:256]
        cs[n, 0] = acc[256:384].astype(jnp.bfloat16)
        cs[n, 1] = acc[384:512].astype(jnp.bfloat16)
        cs_ms[n, 0:1, :] = jnp.where(kept, top * scale, LOWEST)
        cs_ms[n, 1:2, :] = total
        two(cs.at[n], cs_ms.at[n], cr.at[n], cr_ms.at[n], 0, c_recv.at[n], (g_core, j))

    def core_merge(n):
        kx = jnp.where(n < 2 * TILES, xl, 1 - xl)
        arrived(cr.at[n], cr_ms.at[n], c_recv.at[n])
        both = ([own[n, kx], own[n, 1 - kx]], [cr[n, kx], cr[n, 1 - kx]])
        (stay, go), top, total = joined(both[0], cs_ms[n], both[1], cr_ms[n])
        keep[n] = stay
        ps[n] = go.astype(jnp.bfloat16)
        ps_ms[n, 0:1, :] = top
        ps_ms[n, 1:2, :] = total
        two(ps.at[n], ps_ms.at[n], pr.at[n], pr_ms.at[n], 1, p_recv.at[n], (g_pair, j))

    def pair_merge(n):
        step = lax.div(n, TILES)
        tile = lax.rem(n, TILES)
        arrived(pr.at[n], pr_ms.at[n], p_recv.at[n])
        (res,), top, total = joined([keep[n]], ps_ms[n], [pr[n]], pr_ms[n])

        @pl.when(step == 0)
        def _():
            home[tile] = res
            home_ms[tile, 0:1, :] = top
            home_ms[tile, 1:2, :] = total

        @pl.when(step == 1)
        def _():
            hold[tile] = res
            hold_ms[tile, 0:1, :] = top
            hold_ms[tile, 1:2, :] = total

        @pl.when(jnp.logical_and(step == 2, xh == 0))
        def _():
            send_down(res, top, total, 4 + tile)

        @pl.when(jnp.logical_and(step == 2, xh == 1))
        def _():
            send_cross(res, top, total, tile)

        @pl.when(jnp.logical_and(step == 3, xh == 0))
        def _():
            slot = 4 + tile
            arrived(yr.at[slot], yr_ms.at[slot], y_recv.at[slot])
            keep[n] = res
            keep_ms[0:1, :] = top
            keep_ms[1:2, :] = total
            (res2,), top2, total2 = joined([keep[n]], keep_ms, [yr[slot]], yr_ms[slot])
            send_cross(res2, top2, total2, tile)

        @pl.when(jnp.logical_and(step == 3, xh == 1))
        def _():
            send_cross(res, top, total, 4 + tile)

    def late_merge(tile):
        arrived(xr.at[tile], xr_ms.at[tile], x_recv.at[tile])
        (res,), top, total = joined([hold[tile]], hold_ms[tile], [xr[tile]], xr_ms[tile])
        send_down(res, top, total, tile)

    def finish(tile, extra):
        arrived(yr.at[tile], yr_ms.at[tile], y_recv.at[tile])
        if extra:
            slot = 4 + tile
            arrived(xr.at[slot], xr_ms.at[slot], x_recv.at[slot])
            (res,), top, total = joined([home[tile]], home_ms[tile], [xr[slot]], xr_ms[slot])
            home[tile] = res
            home_ms[tile, 0:1, :] = top
            home_ms[tile, 1:2, :] = total
        (res,), top, total = joined([home[tile]], home_ms[tile], [yr[tile]], yr_ms[tile])
        r = res / total
        ratio[tile] = r
        ss[tile] = jnp.broadcast_to(jnp.sum(r * r, axis=0, keepdims=True), ss.shape[1:])
        for d, partner in enumerate((g_core, g_pair, g_both)):
            remote(
                ss.at[tile], sr.at[d, tile], send_sem.at[8 + d], s_recv.at[d, tile], (partner, j)
            ).start()

    def iteration(n, _):
        for step in range(1, STEPS):
            @pl.when(n == TILES * step)
            def _():
                pltpu.make_async_copy(
                    qs.at[step, theirs], qs.at[step, theirs], f_recv.at[step]
                ).wait()

        @pl.when(n < VISITS)
        def _():
            compute(n)

        @pl.when(jnp.logical_and(n >= 1, n < VISITS + 1))
        def _():
            core_merge(n - 1)

        @pl.when(jnp.logical_and(n >= PAIR_LAG, n < VISITS + PAIR_LAG))
        def _():
            pair_merge(n - PAIR_LAG)

        late = 13 + 4 * xh

        @pl.when(jnp.logical_and(n >= late, n < late + TILES))
        def _():
            late_merge(n - late)

        @pl.when(jnp.logical_and(xh == 0, jnp.logical_and(n >= 17, n < 17 + TILES)))
        def _():
            finish(n - 17, True)

        @pl.when(jnp.logical_and(xh == 1, jnp.logical_and(n >= 19, n < 19 + TILES)))
        def _():
            finish(n - 19, False)

        for step in range(1, STEPS):
            @pl.when(n == TILES * step - 2)
            def _():
                pltpu.make_async_copy(
                    qs.at[step, mine], qs.at[step, mine], q_recv.at[step]
                ).wait()
                q_forward(step).start()

        return 0

    lax.fori_loop(0, ITERS, iteration, 0)

    for tile in range(TILES):
        squares = ss[tile, 0:1, :]
        for d in range(3):
            pltpu.make_async_copy(sr.at[d, tile], sr.at[d, tile], s_recv.at[d, tile]).wait()
        squares = (squares + sr[0, tile, 0:1, :]) + (sr[1, tile, 0:1, :] + sr[2, tile, 0:1, :])
        o = ratio[tile] * lax.rsqrt(squares / width + 1e-06)
        out_ref[pl.ds(tile * tq, tq), :] = o.T.astype(jnp.bfloat16)

    def drained(ref, sem):
        pltpu.make_async_copy(ref, ref, send_sem.at[sem]).wait()

    drained(cs, 0)
    drained(cs_ms, 1)
    drained(ps, 2)
    drained(ps_ms, 3)

    @pl.when(xh == 0)
    def _():
        drained(xs.at[pl.ds(0, 4)], 4)
        drained(xs_ms.at[pl.ds(0, 4)], 5)
        drained(ys, 6)
        drained(ys_ms, 7)

    @pl.when(xh == 1)
    def _():
        drained(xs, 4)
        drained(xs_ms, 5)
        drained(ys.at[pl.ds(0, 4)], 6)
        drained(ys_ms.at[pl.ds(0, 4)], 7)

    for d in range(3):
        drained(ss, 8 + d)
    for step in range(1, STEPS):
        q_out[step].wait_send()
        q_forward(step).wait_send()


def attend(skip, keys, vals, queries):
    rows, dk = queries.shape
    window, width = vals.shape
    tq = rows // TILES
    f32, bf16 = jnp.float32, jnp.bfloat16
    vmem = pltpu.VMEM
    dma = pltpu.SemaphoreType.DMA
    share = width // 4

    def both(n, dtype, *lead):
        return [vmem((n, *lead, share, tq), dtype), vmem((n, 2, tq), f32)]

    scratch = [
        vmem((4, share, window), bf16),
        vmem((STEPS, rows, dk), bf16),
        *both(VISITS, f32, 2),
        vmem((VISITS, share, tq), f32),
        vmem((2, tq), f32),
        *both(TILES, f32),
        *both(TILES, f32),
        vmem((TILES, share, tq), f32),
        *both(VISITS, bf16, 2),
        *both(VISITS, bf16, 2),
        *both(VISITS, bf16),
        *both(VISITS, bf16),
        *both(8, bf16),
        *both(8, bf16),
        *both(8, bf16),
        *both(8, bf16),
        vmem((TILES, 8, tq), f32),
        vmem((3, TILES, 8, tq), f32),
        dma((STEPS,)), dma((STEPS,)), dma((STEPS,)), dma((STEPS,)),
        dma((11,)),
        dma((VISITS, 2)), dma((VISITS, 2)), dma((8, 2)), dma((8, 2)), dma((3, TILES)),
    ]
    return pl.pallas_call(
        kernel,
        out_shape=jax.ShapeDtypeStruct((rows, share), bf16),
        in_specs=[
            pl.BlockSpec(memory_space=pltpu.SMEM),
            pl.BlockSpec(memory_space=vmem),
            pl.BlockSpec(memory_space=vmem),
            pl.BlockSpec(memory_space=vmem),
        ],
        out_specs=pl.BlockSpec(memory_space=vmem),
        scratch_shapes=scratch,
        compiler_params=pltpu.CompilerParams(
            collective_id=0, has_side_effects=True, vmem_limit_bytes=56 * 2**20
        ),
    )(skip, keys, vals, queries)


def body(mem_keys, mem_values, offsets, block_skip, queries):
    window = mem_keys.shape[0] // 2
    start = offsets[0, 0]
    keys_w = lax.dynamic_slice_in_dim(mem_keys, start, window, 0)
    vals_w = lax.dynamic_slice_in_dim(mem_values, start, window, 0)
    return attend(block_skip, keys_w, vals_w, queries)


def solution(mesh):
    placed = (
        P(("grp", "blk"), None),
        P(("grp", "blk"), None),
        P("grp", "blk"),
        P("grp", "blk"),
        P("blk", None),
    )
    return jax.shard_map(
        body, mesh=mesh, in_specs=placed, out_specs=P("blk", "grp"), check_vma=False
    )
```

time: 359 us -> 73 us (0.20)
  the two profiles are of different devices: /device:TPU:1 before, /device:TPU:5 now
where the time goes in v1:
time: 73 us; the launch traced here: 72.8 us
  Pallas kernels  65.3 us (89%)
  local copies, waits for them, and re-layouts  6.06 us (8%)
  between operations  1.41 us (2%)
    pallas_call x1, Pallas kernels, attend(): pl.pallas_call(kernel, out_shape=jax.ShapeDtypeStruct((rows, share), bf16...  65.3 us
    dynamic_slice x1, local copies, waits for them, and re-layouts, body(): vals_w = lax.dynamic_slice_in_dim(mem_values, start, window, 0)  3.44 us
    unnamed x3, local copies, waits for them, and re-layouts  1.67 us

profile of v1, /device:TPU:5, one launch (start us, length us, event | category | flops | bytes accessed | tf_op | source)
XLA Modules:
  0.0 72.8 jit_solution(17674670095584577082)
XLA Ops:
  0.0 0.0 copy-start
  1.4 0.0 copy-done
  1.4 0.9 %constant_dynamic-slice_fusion.1.k_ref = bf16[2048,128]{1,0:T(8,128)(2,1)} fusion(bf16[4096,128]{1,0:T(8,128)(2,1)S(1)} %copy-done, s32[]{:T(128)S(6)} %select_n.4), kind=kLoop, calls=%fused_computation.1 | loop fusion | bytes 1048580 | tf_op jit(solution)/shard_map/dynamic_slice | solution.py:356
  2.3 3.4 %constant_dynamic-slice_fusion.v_ref = bf16[2048,512]{1,0:T(8,128)(2,1)} fusion(bf16[4096,512]{1,0:T(8,128)(2,1)} %param.6, s32[]{:T(128)S(6)} %select_n.4), kind=kLoop, calls=%fused_computation | loop fusion | bytes 4194308 | tf_op jit(solution)/shard_map/dynamic_slice | solution.py:357
  5.8 65.3 %shard_map.55 = bf16[1024,128]{1,0:T(8,128)(2,1)} custom-call(s32[1,1]{1,0:T(1,128)S(6)} %copy.8.skip_ref, bf16[2048,128]{1,0:T(8,128)(2,1)} %constant_dynamic-slice_fusion.1.k_ref, bf16[2048,512]{1,0:T(8,128)(2,1)} %constant_dynamic-slice_fusion.v_ref, bf16[1024,128]{1,0:T(8,128)(2,1)} %q_ref.1), custom_call_target="tpu_custom_call" | custom-call | tf_op jit(solution)/shard_map/pallas_call | solution.py:336
  71.1 1.7 %copy.9 = bf16[1024,128]{1,0:T(8,128)(2,1)} copy(bf16[1024,128]{1,0:T(8,128)(2,1)} %shard_map.55) | data formatting | bytes 524288
Async XLA Ops:
  0.0 1.4 %copy-start = (bf16[4096,128]{1,0:T(8,128)(2,1)S(1)}, bf16[4096,128]{1,0:T(8,128)(2,1)}, u32[]{:S(2)}) copy-start(bf16[4096,128]{1,0:T(8,128)(2,1)} %param.5) | copy-start | bytes 3145732

commit v2 on v1

v2 whole, which is shorter than its diff:
```python
import jax
import jax.numpy as jnp
from jax import lax
from jax.experimental import pallas as pl
from jax.experimental.pallas import tpu as pltpu
from jax.sharding import PartitionSpec as P

MESH = pl.DeviceIdType.MESH
LOG2E = 1.4426950408889634
LOWEST = -1e30
HIGHEST = 3e38
TILES = 4
STEPS = 4
VISITS = TILES * STEPS
CHUNKS = 8
HEAD = 3
EARLY = 3
Q_LAG = 3
Q_AHEAD = 4
CORE_LAG = 1
PAIR_LAG = 4
HOP_LAG = 3


def joined(parts):
    tops = [ms[0:1, :] for _, ms in parts]
    top = tops[0]
    for other in tops[1:]:
        top = jnp.maximum(top, other)
    total = None
    sums = None
    for (values, ms), own_top in zip(parts, tops):
        f = jnp.exp2(own_top - top)
        mass = ms[1:2, :] * f
        terms = [v.astype(jnp.float32) * f for v in values]
        total = mass if total is None else total + mass
        sums = terms if sums is None else [a + b for a, b in zip(sums, terms)]
    return sums, top, total


def kernel(
    skip_hbm, start_hbm, k_hbm, v_hbm, q_hbm, out_ref,
    skip_ref, start_ref, k_all, v_all, kw, vt, qs, s_even, s_odd, m_even, m_odd,
    own, keep, home, home_ms, ratio,
    cs, cs_ms, cr, cr_ms, ps, ps_ms, pr, pr_ms,
    es, es_ms, er, er_ms, ds, ds_ms, dr, dr_ms, ss, sr,
    load_sem, q_send, q_recv, f_send, f_recv,
    send_sem, c_recv, p_recv, e_recv, d_recv, s_recv,
):
    g = lax.axis_index("grp")
    j = lax.axis_index("blk")
    nb = lax.axis_size("blk")
    core = lax.rem(g, 2)
    xl = lax.div(g, 2)
    g_core = g + 1 - 2 * core
    g_pair = lax.rem(g + 2, 4)
    g_both = g_core + 2 - 4 * xl

    def at(d):
        return lax.rem(j + nb + d, nb)

    rows = q_hbm.shape[0]
    tq = rows // TILES
    half = tq // 2
    window = kw.shape[0]
    width = v_all.shape[1]
    share = width // 4
    scale = q_hbm.shape[1] ** (-0.5) * LOG2E

    loads = [
        pltpu.make_async_copy(src, dst, load_sem.at[i])
        for i, (src, dst) in enumerate(
            ((start_hbm, start_ref), (skip_hbm, skip_ref), (q_hbm, qs.at[0]), (k_hbm, k_all), (v_hbm, v_all))
        )
    ]
    for load in loads:
        load.start()

    barrier = pltpu.get_barrier_semaphore()
    partners = [
        (g_core, j), (g_pair, j), (g_both, j), (g, at(2)), (g, at(-2)),
        (g_pair, at(1)), (g_pair, at(-1)), (g_pair, at(3)), (g_pair, at(-3)),
    ]
    for partner in partners:
        pl.semaphore_signal(barrier, inc=1, device_id=partner, device_id_type=MESH)

    def remote(src, dst, send, recv, device):
        return pltpu.make_async_remote_copy(
            src_ref=src, dst_ref=dst, send_sem=send, recv_sem=recv,
            device_id=device, device_id_type=MESH,
        )

    homes = {1: (g_pair, at(1)), 2: (g, at(2)), 3: (g_pair, at(3))}

    def q_rows(tile, part):
        return pl.ds(tile * tq + part * half, half)

    def q_copy(back, tile):
        return remote(
            qs.at[0, q_rows(tile, core)], qs.at[back, q_rows(tile, core)],
            q_send.at[back], q_recv.at[back, tile], homes[back],
        )

    def q_forward(back, tile):
        piece = qs.at[back, q_rows(tile, core)]
        pltpu.make_async_copy(piece, piece, q_recv.at[back, tile]).wait()
        remote(piece, piece, f_send.at[back], f_recv.at[back, tile], (g_core, j)).start()

    def q_wait(back, tile):
        piece = qs.at[back, q_rows(tile, 1 - core)]
        pltpu.make_async_copy(piece, piece, f_recv.at[back, tile]).wait()

    for load in loads[:4]:
        load.wait()
    start = start_ref[0, 0]

    def windowed(ref, begin, size):
        low = ref[begin : begin + size, :].astype(jnp.float32)
        high = ref[window + begin : window + begin + size, :].astype(jnp.float32)
        row = begin + lax.broadcasted_iota(jnp.int32, low.shape, 0)
        return jnp.where(row >= start, low, high).astype(jnp.bfloat16)

    piece_rows = window // 8
    for c in range(8):
        kw[c * piece_rows : (c + 1) * piece_rows, :] = windowed(k_all, c * piece_rows, piece_rows)
    loads[4].wait()
    for c in range(8):
        piece = windowed(v_all, c * piece_rows, piece_rows)
        for q in range(4):
            spot = 2 * lax.rem(core + q % 2, 2) + q // 2
            vt[spot, :, c * piece_rows : (c + 1) * piece_rows] = piece[
                :, q * share : (q + 1) * share
            ].T

    def two(data_src, ms_src, data_dst, ms_dst, sem, recv, device):
        remote(data_src, data_dst, send_sem.at[2 * sem], recv.at[0], device).start()
        remote(ms_src, ms_dst, send_sem.at[2 * sem + 1], recv.at[1], device).start()

    def arrived(data, ms, recv):
        pltpu.make_async_copy(data, data, recv.at[0]).wait()
        pltpu.make_async_copy(ms, ms, recv.at[1]).wait()

    def visit(n):
        m = n - HEAD
        phase = lax.div(m + 4, 4) - 1
        remote_visit = jnp.logical_and(m >= 0, m < 12)
        back = jnp.where(phase == 2, 1, phase + 2)
        back = jnp.where(remote_visit, back, 0)
        tile = jnp.where(remote_visit, m - 4 * phase, jnp.where(m < 0, n, n - 12))
        return back, tile

    def scores(n, s_ref, c, chunk, q):
        part = slice(c * chunk, (c + 1) * chunk)
        s = lax.dot_general(
            kw[part, :], q, (((1,), (1,)), ((), ())), preferred_element_type=jnp.float32
        )
        s_ref[part, :] = s
        return jnp.max(s, axis=0, keepdims=True)

    def queries_of(n):
        back, tile = visit(n)
        return qs[back, pl.ds(pl.multiple_of(tile * tq, tq), tq), :]

    chunk = window // CHUNKS

    def compute(n, s_now, m_now, s_next, m_next):
        back, _ = visit(n)
        kept = skip_ref[0, 0] != lax.rem(j + nb - back, nb)
        q = queries_of(jnp.minimum(n + 1, VISITS - 1))
        top = m_now[0:1, :]
        ref = jnp.where(kept, top, HIGHEST)
        high = total = None
        probs = []
        for c in range(CHUNKS):
            part = slice(c * chunk, (c + 1) * chunk)
            peak = scores(n, s_next, c, chunk, q)
            high = peak if high is None else jnp.maximum(high, peak)
            p = jnp.exp2((s_now[part, :] - ref) * scale)
            mass = jnp.sum(p, axis=0, keepdims=True)
            total = mass if total is None else total + mass
            probs.append(p.astype(jnp.bfloat16))
        m_next[0:1, :] = high
        acc = jnp.dot(
            vt[...].reshape(width, window), jnp.concatenate(probs, axis=0),
            preferred_element_type=jnp.float32,
        )
        own[n, 0] = acc[0:share]
        own[n, 1] = acc[share : 2 * share]
        cs[n, 0] = acc[2 * share : 3 * share].astype(jnp.bfloat16)
        cs[n, 1] = acc[3 * share : 4 * share].astype(jnp.bfloat16)
        cs_ms[n, 0:1, :] = jnp.where(kept, top * scale, LOWEST)
        cs_ms[n, 1:2, :] = total
        two(cs.at[n], cs_ms.at[n], cr.at[n], cr_ms.at[n], 0, c_recv.at[n], (g_core, j))

    def core_merge(n):
        back, tile = visit(n)
        kx = jnp.where(lax.rem(back, 2) == 0, xl, 1 - xl)
        late = tile >= EARLY
        slot = jnp.maximum(tile - EARLY, 0)
        arrived(cr.at[n], cr_ms.at[n], c_recv.at[n])

        def chip(a, b):
            return [
                ([own[n, a], own[n, b]], cs_ms[n]),
                ([cr[n, a], cr[n, b]], cr_ms[n]),
            ]

        def to_pair(parts):
            (stay, go), top, total = joined(parts)
            keep[n] = stay
            ps[n] = go.astype(jnp.bfloat16)
            ps_ms[n, 0:1, :] = top
            ps_ms[n, 1:2, :] = total
            two(ps.at[n], ps_ms.at[n], pr.at[n], pr_ms.at[n], 1, p_recv.at[n], (g_pair, j))

        @pl.when(jnp.logical_not(jnp.logical_and(late, lax.rem(back, 2) == 0)))
        def _():
            to_pair(chip(kx, 1 - kx))

        @pl.when(jnp.logical_and(late, back == 0))
        def _():
            arrived(er.at[slot], er_ms.at[slot], e_recv.at[slot])
            more = ([er[slot, kx], er[slot, 1 - kx]], er_ms[slot])
            to_pair(chip(kx, 1 - kx) + [more])

        @pl.when(jnp.logical_and(late, back == 2))
        def _():
            (low, high), top, total = joined(chip(0, 1))
            es[slot, 0] = low.astype(jnp.bfloat16)
            es[slot, 1] = high.astype(jnp.bfloat16)
            es_ms[slot, 0:1, :] = top
            es_ms[slot, 1:2, :] = total
            two(
                es.at[slot], es_ms.at[slot], er.at[slot], er_ms.at[slot], 2, e_recv.at[slot],
                (g, at(-2)),
            )

    def pair_merge(n):
        back, tile = visit(n)

        def paired():
            arrived(pr.at[n], pr_ms.at[n], p_recv.at[n])
            (res,), top, total = joined([([keep[n]], ps_ms[n]), ([pr[n]], pr_ms[n])])
            return res, top, total

        @pl.when(back == 0)
        def _():
            res, top, total = paired()
            home[tile] = res
            home_ms[tile, 0:1, :] = top
            home_ms[tile, 1:2, :] = total

        def send_home(b):
            res, top, total = paired()
            ds[b - 1, tile] = res.astype(jnp.bfloat16)
            ds_ms[b - 1, tile, 0:1, :] = top
            ds_ms[b - 1, tile, 1:2, :] = total
            two(
                ds.at[b - 1, tile], ds_ms.at[b - 1, tile], dr.at[b - 1, tile],
                dr_ms.at[b - 1, tile], 2 + b, d_recv.at[b - 1, tile],
                (g if b == 2 else g_pair, at(-b)),
            )

        for b in (1, 3):
            @pl.when(back == b)
            def _():
                send_home(b)

        @pl.when(jnp.logical_and(back == 2, tile < EARLY))
        def _():
            send_home(2)

    def finish(tile):
        def collect(backs):
            for b in backs:
                arrived(dr.at[b - 1, tile], dr_ms.at[b - 1, tile], d_recv.at[b - 1, tile])
            (res,), _, total = joined(
                [([home[tile]], home_ms[tile])]
                + [([dr[b - 1, tile]], dr_ms[b - 1, tile]) for b in backs]
            )
            r = res / total
            ratio[tile] = r
            ss[tile] = jnp.broadcast_to(jnp.sum(r * r, axis=0, keepdims=True), ss.shape[1:])

        @pl.when(tile < EARLY)
        def _():
            collect((1, 2, 3))

        @pl.when(tile >= EARLY)
        def _():
            collect((1, 3))

        for d, partner in enumerate((g_core, g_pair, g_both)):
            remote(
                ss.at[tile], sr.at[d, tile], send_sem.at[12 + d], s_recv.at[d, tile], (partner, j)
            ).start()

    def send_visit(n):
        back, tile = visit(n)
        for b in range(1, STEPS):
            @pl.when(back == b)
            def _():
                q_copy(b, tile).start()

    def forward_visit(n):
        back, tile = visit(n)
        for b in range(1, STEPS):
            @pl.when(back == b)
            def _():
                q_forward(b, tile)

    def wait_visit(n):
        back, tile = visit(n)

        @pl.when(back > 0)
        def _():
            q_wait(back, tile)

    def iteration(n, s_now, m_now, s_next, m_next):
        @pl.when(n < 12 - Q_AHEAD)
        def _():
            send_visit(n + HEAD + Q_AHEAD)

        @pl.when(n < VISITS - 1)
        def _():
            wait_visit(n + 1)

        @pl.when(n < VISITS)
        def _():
            compute(n, s_now, m_now, s_next, m_next)

        @pl.when(n < VISITS - Q_LAG)
        def _():
            forward_visit(n + Q_LAG)

        @pl.when(jnp.logical_and(n >= CORE_LAG, n < VISITS + CORE_LAG))
        def _():
            core_merge(n - CORE_LAG)

        @pl.when(jnp.logical_and(n >= PAIR_LAG, n < VISITS + PAIR_LAG))
        def _():
            pair_merge(n - PAIR_LAG)

        last = HEAD + 8 + PAIR_LAG + HOP_LAG

        @pl.when(jnp.logical_and(n >= last, n < last + TILES))
        def _():
            finish(n - last)

    q0 = queries_of(0)
    high = None
    for c in range(CHUNKS):
        peak = scores(0, s_even, c, chunk, q0)
        high = peak if high is None else jnp.maximum(high, peak)
    m_even[0:1, :] = high

    pl.semaphore_wait(barrier, len(partners))
    for tile in range(Q_AHEAD):
        q_copy(2, tile).start()

    def two_iterations(u, _):
        iteration(2 * u, s_even, m_even, s_odd, m_odd)
        iteration(2 * u + 1, s_odd, m_odd, s_even, m_even)
        return 0

    last_iteration = HEAD + 8 + PAIR_LAG + HOP_LAG + TILES
    lax.fori_loop(0, (last_iteration + 1) // 2, two_iterations, 0)

    for tile in range(TILES):
        squares = ss[tile, 0:1, :]
        for d in range(3):
            pltpu.make_async_copy(sr.at[d, tile], sr.at[d, tile], s_recv.at[d, tile]).wait()
        squares = (squares + sr[0, tile, 0:1, :]) + (sr[1, tile, 0:1, :] + sr[2, tile, 0:1, :])
        o = ratio[tile] * lax.rsqrt(squares / width + 1e-06)
        out_ref[pl.ds(tile * tq, tq), :] = o.T.astype(jnp.bfloat16)

    def drained(ref, sem):
        pltpu.make_async_copy(ref, ref, send_sem.at[sem]).wait()

    drained(cs, 0)
    drained(cs_ms, 1)
    paired = pl.ds(0, VISITS - (TILES - EARLY))
    drained(ps.at[paired], 2)
    drained(ps_ms.at[paired], 3)
    drained(es, 4)
    drained(es_ms, 5)
    for b in range(1, STEPS):
        count = EARLY if b == 2 else TILES
        drained(ds.at[b - 1, pl.ds(0, count)], 2 * (2 + b))
        drained(ds_ms.at[b - 1, pl.ds(0, count)], 2 * (2 + b) + 1)
    for d in range(3):
        drained(ss, 12 + d)
    sent = qs.at[0, pl.ds(0, rows // 2)]
    for back in range(1, STEPS):
        pltpu.make_async_copy(sent, sent, q_send.at[back]).wait()
        pltpu.make_async_copy(sent, sent, f_send.at[back]).wait()


def attend(skip, start, mem_keys, mem_values, queries):
    rows, dk = queries.shape
    resident, width = mem_values.shape
    window = resident // 2
    tq = rows // TILES
    f32, bf16 = jnp.float32, jnp.bfloat16
    vmem = pltpu.VMEM
    dma = pltpu.SemaphoreType.DMA
    share = width // 4

    def both(n, dtype, *lead):
        return [vmem((n, *lead, share, tq), dtype), vmem((n, 2, tq), f32)]

    scratch = [
        pltpu.SMEM((1, 1), jnp.int32),
        pltpu.SMEM((1, 1), jnp.int32),
        vmem((resident, dk), bf16),
        vmem((resident, width), bf16),
        vmem((window, dk), bf16),
        vmem((4, share, window), bf16),
        vmem((STEPS, rows, dk), bf16),
        vmem((window, tq), f32),
        vmem((window, tq), f32),
        vmem((8, tq), f32),
        vmem((8, tq), f32),
        vmem((VISITS, 2, share, tq), f32),
        vmem((VISITS, share, tq), f32),
        *both(TILES, f32),
        vmem((TILES, share, tq), f32),
        *both(VISITS, bf16, 2),
        *both(VISITS, bf16, 2),
        *both(VISITS, bf16),
        *both(VISITS, bf16),
        *both(TILES - EARLY, bf16, 2),
        *both(TILES - EARLY, bf16, 2),
        vmem((3, TILES, share, tq), bf16),
        vmem((3, TILES, 2, tq), f32),
        vmem((3, TILES, share, tq), bf16),
        vmem((3, TILES, 2, tq), f32),
        vmem((TILES, 8, tq), f32),
        vmem((3, TILES, 8, tq), f32),
        dma((5,)),
        dma((STEPS,)), dma((STEPS, TILES)), dma((STEPS,)), dma((STEPS, TILES)),
        dma((15,)),
        dma((VISITS, 2)), dma((VISITS, 2)), dma((TILES - EARLY, 2)), dma((3, TILES, 2)),
        dma((3, TILES)),
    ]
    return pl.pallas_call(
        kernel,
        out_shape=jax.ShapeDtypeStruct((rows, share), bf16),
        in_specs=[
            pl.BlockSpec(memory_space=pl.ANY) for _ in range(5)
        ],
        out_specs=pl.BlockSpec(memory_space=vmem),
        scratch_shapes=scratch,
        compiler_params=pltpu.CompilerParams(
            collective_id=0, has_side_effects=True, vmem_limit_bytes=56 * 2**20
        ),
    )(skip, start, mem_keys, mem_values, queries)


def body(mem_keys, mem_values, offsets, block_skip, queries):
    return attend(block_skip, offsets, mem_keys, mem_values, queries)


def solution(mesh):
    placed = (
        P(("grp", "blk"), None),
        P(("grp", "blk"), None),
        P("grp", "blk"),
        P("grp", "blk"),
        P("blk", None),
    )
    return jax.shard_map(
        body, mesh=mesh, in_specs=placed, out_specs=P("blk", "grp"), check_vma=False
    )
```

time: 73 us -> 51.7 us (0.71)
  the two profiles are of different devices: /device:TPU:5 before, /device:TPU:1 now
where the time goes in v2:
time: 51.7 us; the launch traced here: 51.5 us
  Pallas kernels  48.6 us (94%)
  local copies, waits for them, and re-layouts  1.67 us (3%)
  between operations  1.3 us (3%)
    pallas_call x1, Pallas kernels, attend(): pl.pallas_call(kernel, out_shape=jax.ShapeDtypeStruct((rows, share), bf16...  48.6 us
    unnamed x1, local copies, waits for them, and re-layouts  1.67 us

profile of v2, /device:TPU:1, one launch (start us, length us, event | category | flops | bytes accessed | tf_op | source)
XLA Modules:
  0.0 51.5 jit_solution(7913003367962974408)
XLA Ops:
  1.3 48.6 %shard_map.55 = bf16[1024,128]{1,0:T(8,128)(2,1)} custom-call(s32[1,1]{1,0:T(1,128)S(6)} %copy.8.skip_hbm, s32[1,1]{1,0:T(1,128)S(6)} %copy.7.start_hbm, bf16[4096,128]{1,0:T(8,128)(2,1)} %k_hbm.1, bf16[4096,512]{1,0:T(8,128)(2,1)} %v_hbm.1, bf16[1024,128]{1,0:T(8,128)(2,1)} %q_hbm.1), custom_call_target="tpu_custom_call" | custom-call | tf_op jit(solution)/shard_map/pallas_call | solution.py:446
  49.9 1.7 %copy.9 = bf16[1024,128]{1,0:T(8,128)(2,1)} copy(bf16[1024,128]{1,0:T(8,128)(2,1)} %shard_map.55) | data formatting | bytes 524288

commit v3 on v2

--- a/solution.py
+++ b/solution.py
@@ -110,8 +110,12 @@
         piece = qs.at[back, q_rows(tile, 1 - core)]
         pltpu.make_async_copy(piece, piece, f_recv.at[back, tile]).wait()
 
-    for load in loads[:4]:
+    for load in loads[:3]:
         load.wait()
+    pl.semaphore_wait(barrier, len(partners))
+    for tile in range(Q_AHEAD):
+        q_copy(2, tile).start()
+    loads[3].wait()
     start = start_ref[0, 0]
 
     def windowed(ref, begin, size):
@@ -329,17 +333,21 @@
         def _():
             compute(n, s_now, m_now, s_next, m_next)
 
+        @pl.when(n == 0)
+        def _():
+            core_merge(n)
+
+        @pl.when(jnp.logical_and(n >= CORE_LAG + 1, n < VISITS + CORE_LAG))
+        def _():
+            core_merge(n - CORE_LAG)
+
+        @pl.when(jnp.logical_and(n >= PAIR_LAG, n < VISITS + PAIR_LAG))
+        def _():
+            pair_merge(n - PAIR_LAG)
+
         @pl.when(n < VISITS - Q_LAG)
         def _():
             forward_visit(n + Q_LAG)
-
-        @pl.when(jnp.logical_and(n >= CORE_LAG, n < VISITS + CORE_LAG))
-        def _():
-            core_merge(n - CORE_LAG)
-
-        @pl.when(jnp.logical_and(n >= PAIR_LAG, n < VISITS + PAIR_LAG))
-        def _():
-            pair_merge(n - PAIR_LAG)
 
         last = HEAD + 8 + PAIR_LAG + HOP_LAG
 
@@ -353,10 +361,6 @@
         peak = scores(0, s_even, c, chunk, q0)
         high = peak if high is None else jnp.maximum(high, peak)
     m_even[0:1, :] = high
-
-    pl.semaphore_wait(barrier, len(partners))
-    for tile in range(Q_AHEAD):
-        q_copy(2, tile).start()
 
     def two_iterations(u, _):
         iteration(2 * u, s_even, m_even, s_odd, m_odd)

time: 51.7 us -> 50.1 us (0.969); the launches traced: 51.5 us -> 49.2 us
  Pallas kernels: 48.6 us -> 46.2 us
    pallas_call x1, Pallas kernels: 48.6 us -> 46.2 us  [attend(): pl.pallas_call(kernel, out_shape=jax.ShapeDtypeStruct((rows, share), bf16...]
where the time goes in v3:
time: 50.1 us; the launch traced here: 49.2 us
  Pallas kernels  46.2 us (92%)
  local copies, waits for them, and re-layouts  1.67 us (3%)
  between operations  1.3 us (3%)
    pallas_call x1, Pallas kernels, attend(): pl.pallas_call(kernel, out_shape=jax.ShapeDtypeStruct((rows, share), bf16...  46.2 us
    unnamed x1, local copies, waits for them, and re-layouts  1.67 us

profile of v3, /device:TPU:1, one launch (start us, length us, event | category | flops | bytes accessed | tf_op | source)
XLA Modules:
  0.0 49.2 jit_solution(6606648735583041403)
XLA Ops:
  1.3 46.2 %shard_map.55 = bf16[1024,128]{1,0:T(8,128)(2,1)} custom-call(s32[1,1]{1,0:T(1,128)S(6)} %copy.8.skip_hbm, s32[1,1]{1,0:T(1,128)S(6)} %copy.7.start_hbm, bf16[4096,128]{1,0:T(8,128)(2,1)} %k_hbm.1, bf16[4096,512]{1,0:T(8,128)(2,1)} %v_hbm.1, bf16[1024,128]{1,0:T(8,128)(2,1)} %q_hbm.1), custom_call_target="tpu_custom_call" | custom-call | tf_op jit(solution)/shard_map/pallas_call | solution.py:450
  47.5 1.7 %copy.9 = bf16[1024,128]{1,0:T(8,128)(2,1)} copy(bf16[1024,128]{1,0:T(8,128)(2,1)} %shard_map.55) | data formatting | bytes 524288
